TPU v7x, 256 devices: a whole 4x4x8 slice. The times are simulated.
256 devices in a mesh: ctx: 32 (over z, x), head: 8 (over y, core).
Axes of the slice: x: 4, y: 4, z: 8, core: 2. Of those that a mesh axis runs over, the one named last changes fastest.
Arguments:
- queries: bfloat16 [98304, 1024], P('ctx', 'head'), may hold values from -6 to 6
- keys: bfloat16 [98304, 1024], P('ctx', 'head'), may hold values from -6 to 6
- values: bfloat16 [98304, 1024], P('ctx', 'head'), may hold values from -6 to 6
- prefix: int32 [1], replicated, may hold values from 24576 to 73727
- norm_gain: float32 [1024], P('head'), may hold values from 0.1 to 1.9
- out_weight: bfloat16 [1024, 4096], P(None, 'head'), may hold values from -0.1875 to 0.1875
Outputs:
- projected: bfloat16 [98304, 4096], P('ctx', 'head')
All inputs are finite; a program needn't handle non-finite values.
Results may differ from a plain program's by a relative error of at most 0.0049.
Values may be sent and summed in bfloat16 or wider, within the bound.
A program may use at most 64 MiB of HBM per device.

v0:
```python
import jax
import jax.numpy as jnp
from jax import lax
from jax.sharding import PartitionSpec as P

HD = 128
GROUP = 512


def prefix_2(part, axis, combine, identity):
    place = lax.axis_index(axis)
    gathered = lax.all_gather(part, axis)
    state = jnp.zeros_like(part) + jnp.asarray(identity, part.dtype)

    def one(hop, state):
        return combine(state, lax.dynamic_index_in_dim(gathered, hop, 0, False))

    return lax.fori_loop(0, place, one, state)


def add_states(preceding_tokens, later):
    return preceding_tokens + later


def body(queries, keys, values, prefix, norm_gain, out_weight):
    row_count, feature_dimension = queries.shape
    local_heads = feature_dimension // HD
    blocks = row_count // GROUP
    leading_token = lax.axis_index("ctx") * row_count
    positions = leading_token + jnp.arange(row_count, dtype=jnp.int32)
    inside = (positions < prefix[0]).reshape(blocks, GROUP)
    query_blocks = queries.reshape(blocks, GROUP, local_heads, HD)
    key_blocks = keys.reshape(blocks, GROUP, local_heads, HD)
    value_blocks = values.reshape(blocks, GROUP, local_heads, HD)
    block_states = jnp.einsum(
        "nchd,nche->nhde", key_blocks, value_blocks, preferred_element_type=jnp.float32
    )
    masked_keys = key_blocks * inside[:, :, None, None].astype(jnp.bfloat16)
    masked_state = jnp.sum(
        jnp.einsum(
            "nchd,nche->nhde", masked_keys, value_blocks, preferred_element_type=jnp.float32
        ),
        axis=0,
    )
    local_state = jnp.sum(block_states, axis=0)
    carried = prefix_2(local_state, "ctx", add_states, jnp.zeros_like(local_state))
    prefix_state = lax.psum(masked_state, "ctx")
    running = jnp.cumsum(block_states, axis=0)
    prior = carried[None] + jnp.concatenate(
        [jnp.zeros_like(block_states[:1]), running[:-1]], axis=0
    )
    whole_inside = inside[:, -1]
    chosen_state = jnp.where(whole_inside[:, None, None, None], prefix_state[None], prior)
    query_as_float = query_blocks.astype(jnp.float32)
    preceding_tokens = jnp.einsum(
        "nchd,nhde->nche", query_as_float, chosen_state, precision=lax.Precision.HIGHEST
    )
    straddle = jnp.clip((prefix[0] - leading_token) // GROUP, 0, blocks - 1)
    straddle_query = lax.dynamic_slice_in_dim(query_as_float, straddle, 1, 0)
    straddle_read = jnp.einsum(
        "nchd,hde->nche", straddle_query, prefix_state, precision=lax.Precision.HIGHEST
    )
    prefix_fill = lax.dynamic_update_slice_in_dim(preceding_tokens, straddle_read, straddle, 0)
    attention_scores = jnp.einsum(
        "nchd,nmhd->nhcm", query_blocks, key_blocks, preferred_element_type=jnp.float32
    )
    lower_mask = jnp.tril(jnp.ones((GROUP, GROUP), dtype=bool))
    weights = jnp.where(lower_mask[None, None], attention_scores, 0.0).astype(jnp.bfloat16)
    local_part = jnp.einsum(
        "nhcm,nmhe->nche", weights, value_blocks, preferred_element_type=jnp.float32
    )
    attended = jnp.where(inside[:, :, None, None], prefix_fill, preceding_tokens + local_part)
    mean_square = jnp.mean(attended * attended, axis=-1, keepdims=True)
    head_normalized = attended * lax.rsqrt(mean_square + 1e-06) * norm_gain.reshape(local_heads, HD)
    head_normalized = head_normalized.astype(jnp.bfloat16).reshape(row_count, feature_dimension)
    projected = jnp.dot(
        lax.all_gather(head_normalized, "head", axis=1, tiled=True),
        out_weight,
        preferred_element_type=jnp.float32,
    )
    return projected.astype(jnp.bfloat16)


def solution(mesh):
    return jax.shard_map(
        body,
        mesh=mesh,
        in_specs=(
            P("ctx", "head"),
            P("ctx", "head"),
            P("ctx", "head"),
            P(),
            P("head"),
            P(None, "head"),
        ),
        out_specs=P("ctx", "head"),
        check_vma=False,
    )
```

profile of v0, /device:TPU:1, one launch (start us, length us, event | category | flops | bytes accessed | tf_op | source)
XLA Modules:
  0.0 305.3 jit_solution(16947940067111918171)
XLA Ops:
  6.5 0.0 copy-start
  6.5 0.0 copy-start.2
  6.5 0.0 copy-start.1
  6.5 0.0 all-gather.6.cloned.1.call-start
  6.5 2.6 fusion.24
  9.1 0.0 all-gather.6.cloned.1.call-update
  9.1 0.0 all-reduce.3.cloned.1.call-start
  9.9 0.0 copy-done.2
  9.9 0.0 copy-done.1
  9.9 1.5 convolution_bitcast_fusion.2
  11.4 0.0 all-reduce.3.cloned.1.call-update
  11.4 0.0 all-gather.4.cloned.1.call-start
  11.5 0.1 iota_compare_fusion
  11.6 0.2 slice_reduce_fusion
  11.8 0.3 fusion.9
  12.1 75.6 %all-gather.6.cloned.1.call-done = f32[4096,128]{1,0:T(8,128)} async-done(((f32[128,128]{1,0:T(8,128)}), f32[4096,128]{1,0:T(8,128)}) %all-gather.6.cloned.1.call-update) | async-done | bytes 2097168 | tf_op jit(solution)/shard_map/all_gather | solution.py:12
  87.8 139.6 %all-reduce.3.cloned.1.call-done = f32[128,128]{1,0:T(8,128)} async-done(((f32[128,128]{1,0:T(8,128)}), f32[128,128]{1,0:T(8,128)}) %all-reduce.3.cloned.1.call-update) | async-done | bytes 65552 | tf_op jit(solution)/shard_map/psum | solution.py:47
  227.4 2.1 convolution_bitcast_fusion
  229.5 0.0 copy-start.3
  229.5 1.1 copy.41
  230.6 0.0 copy-done.3
  230.6 1.9 fusion.6
  232.6 0.0 copy-start.4
  232.6 5.3 %multiply_reduce_fusion = (f32[6,512]{1,0:T(8,128)S(1)}, f32[6,512,1,128]{1,3,0,2:T(8,128)}) fusion(f32[6,512,1,128]{1,3,0,2:T(8,128)} %fusion.6, f32[6,512,1,128]{1,3,0,2:T(8,128)S(1)} %convolution_bitcast_fusion, bf16[6,512,128]{2,1,0:T(8,128)(2,1)} %bitcast.63, pred[512,512]{1,0:T(8,128)(4,1)S(1)} %iota_compare_fusion, ...), kind=kOutput, calls=%fused_computation.10 | convolution fusion | flops 810021888 | bytes 7355392 | tf_op jit(solution)/shard_map/nhcm,nmhe->nche/dot_general | solution.py:69
  237.8 0.0 copy-done.4
  237.9 1.8 multiply_convert_fusion
  239.6 1.2 copy.29
  240.8 0.0 all-gather.4.cloned.1.call-update
  240.8 50.4 %all-gather.4.cloned.1.call-done = bf16[3072,1024]{1,0:T(8,128)(2,1)} async-done(((bf16[3072,128]{1,0:T(8,128)(2,1)}), bf16[3072,1024]{1,0:T(8,128)(2,1)}) %all-gather.4.cloned.1.call-update) | async-done | bytes 6291472 | tf_op jit(solution)/shard_map/all_gather | solution.py:77
  291.2 0.0 copy-done
  291.2 7.5 %convolution_convert_fusion = bf16[3072,512]{1,0:T(8,128)(2,1)} fusion(bf16[3072,1024]{1,0:T(8,128)(2,1)} %all-gather.4.cloned.1.call-done, bf16[1024,512]{1,0:T(8,128)(2,1)S(1)} %copy-done), kind=kOutput, calls=%fused_computation.2 | convolution fusion | flops 3222798336 | bytes 10485760 | tf_op jit(solution)/shard_map/dot_general | solution.py:76
  (6 shorter events, 0.1 us)
Async XLA Ops:
  6.5 284.7 %copy-start = (bf16[1024,512]{1,0:T(8,128)(2,1)S(1)}, bf16[1024,512]{1,0:T(8,128)(2,1)}, u32[]{:S(2)}) copy-start(bf16[1024,512]{1,0:T(8,128)(2,1)} %param.13) | copy-start | bytes 3145732
  6.5 3.3 %copy-start.2 = (bf16[3072,128]{1,0:T(8,128)(2,1)S(1)}, bf16[3072,128]{1,0:T(8,128)(2,1)}, u32[]{:S(2)}) copy-start(bf16[3072,128]{1,0:T(8,128)(2,1)} %param.10) | copy-start | bytes 2359300
  6.5 3.3 %copy-start.1 = (bf16[3072,128]{1,0:T(8,128)(2,1)S(1)}, bf16[3072,128]{1,0:T(8,128)(2,1)}, u32[]{:S(2)}) copy-start(bf16[3072,128]{1,0:T(8,128)(2,1)} %param.9) | copy-start | bytes 2359300
  6.5 81.2 %all-gather.6.cloned.1.call-start = ((), (), s32[]{:S(2)}) async-start(), calls=%async_computation.2 | async-start | bytes 2162688 | tf_op jit(solution)/shard_map/all_gather | solution.py:12
  9.1 218.3 %all-reduce.3.cloned.1.call-start = ((), (), s32[]{:S(2)}) async-start(), calls=%async_computation | async-start | bytes 131072 | tf_op jit(solution)/shard_map/psum | solution.py:47
  11.4 279.8 %all-gather.4.cloned.1.call-start = ((), (), s32[]{:S(2)}) async-start(), calls=%async_computation.1 | async-start | bytes 7077888 | tf_op jit(solution)/shard_map/all_gather | solution.py:77
  229.5 1.2 copy-start.3
  232.6 5.3 %copy-start.4 = (f32[128]{0:T(128)S(1)}, f32[128]{0:T(128)}, u32[]{:S(2)}) copy-start(f32[128]{0:T(128)} %param.12) | copy-start | bytes 1540
Sparse Core Ops, SparseCore 0:
  9.9 77.7 all-gather.5
  91.2 136.1 all-reduce.2
  240.9 50.2 all-gather.3
where the time goes:
time: 307 us; the launch traced here: 305 us
  waiting for transfers between devices  266 us (87%)
  matrix products  20.9 us (7%)
  between operations  13.9 us (5%)
    psum x1, waiting for transfers between devices, body(): prefix_state = lax.psum(masked_state, 'ctx')  140 us
    all_gather x1, waiting for transfers between devices, prefix_2(): gathered = lax.all_gather(part, axis)  75.6 us
    all_gather x1, waiting for transfers between devices, body(): lax.all_gather(head_normalized, 'head', axis=1, tiled=True)  50.4 us
    dot_general x1, matrix products, body(): jnp.dot(lax.all_gather(head_normalized, 'head', axis=1, tiled=True), out_...  7.54 us
  transfers between devices with their start and end apart: 3, of which 3 were waited for; matrix products, arithmetic and copies ran while one was open for 1% of the time, Pallas kernels for 0%

commit v1 on v0

--- a/solution.py
+++ b/solution.py
@@ -44,7 +44,7 @@
     )
     local_state = jnp.sum(block_states, axis=0)
     carried = prefix_2(local_state, "ctx", add_states, jnp.zeros_like(local_state))
-    prefix_state = lax.psum(masked_state, "ctx")
+    prefix_state = jnp.sum(lax.all_gather(masked_state, "ctx"), axis=0)
     running = jnp.cumsum(block_states, axis=0)
     prior = carried[None] + jnp.concatenate(
         [jnp.zeros_like(block_states[:1]), running[:-1]], axis=0

time: 307 us -> 270 us (0.88)
  waiting for transfers between devices: 266 us -> 227 us
    psum x1 -> x0, waiting for transfers between devices: 140 us -> none  [body(): prefix_state = lax.psum(masked_state, 'ctx')]
    all_gather x0 -> x1, waiting for transfers between devices: none -> 76.1 us  [body(): prefix_state = jnp.sum(lax.all_gather(masked_state, 'ctx'), axis=0)]
    all_gather x1, waiting for transfers between devices: 50.4 us -> 74.9 us  [body(): lax.all_gather(head_normalized, 'head', axis=1, tiled=True)]
where the time goes in v1:
time: 270 us; the launch traced here: 268 us
  waiting for transfers between devices  227 us (84%)
  matrix products  20.7 us (8%)
  between operations  14 us (5%)
  other arithmetic  3.87 us (1%)
    all_gather x1, waiting for transfers between devices, body(): prefix_state = jnp.sum(lax.all_gather(masked_state, 'ctx'), axis=0)  76.1 us
    all_gather x1, waiting for transfers between devices, prefix_2(): gathered = lax.all_gather(part, axis)  76 us
    all_gather x1, waiting for transfers between devices, body(): lax.all_gather(head_normalized, 'head', axis=1, tiled=True)  74.9 us
    dot_general x1, matrix products, body(): jnp.dot(lax.all_gather(head_normalized, 'head', axis=1, tiled=True), out_...  7.54 us
  transfers between devices with their start and end apart: 3, of which 3 were waited for; matrix products, arithmetic and copies ran while one was open for 1% of the time, Pallas kernels for 0%

profile of v1, /device:TPU:1, one launch (start us, length us, event | category | flops | bytes accessed | tf_op | source)
XLA Modules:
  0.0 268.2 jit_solution(4028617576486628699)
XLA Ops:
  6.5 0.0 copy-start
  6.5 0.0 copy-start.1
  6.5 0.0 copy-start.2
  6.5 0.0 all-gather.8.cloned.1.call-start
  7.4 2.9 %convolution_bitcast_fusion.2 = f32[128,128]{1,0:T(8,128)} fusion(bf16[6,512,128]{2,1,0:T(8,128)(2,1)} %bitcast.61, bf16[6,512,128]{2,1,0:T(8,128)(2,1)} %bitcast.64, bf16[6,512]{1,0:T(8,128)(2,1)S(1)} %fusion.20), kind=kOutput, calls=%fused_computation.14 | convolution fusion | flops 101056512 | bytes 1644544 | tf_op jit(solution)/shard_map/nchd,nche->nhde/dot_general | solution.py:40
  10.3 0.0 all-gather.8.cloned.1.call-update
  10.3 0.0 all-gather.10.cloned.1.call-start
  10.3 0.0 copy-done.1
  10.3 0.0 copy-done.2
  10.4 1.0 fusion.24
  11.4 0.0 all-gather.10.cloned.1.call-update
  11.4 0.0 all-gather.6.cloned.1.call-start
  11.5 0.3 fusion.9
  11.9 0.2 slice_reduce_fusion
  12.0 0.1 iota_compare_fusion
  12.1 76.1 %all-gather.8.cloned.1.call-done = f32[4096,128]{1,0:T(8,128)} async-done(((f32[128,128]{1,0:T(8,128)}), f32[4096,128]{1,0:T(8,128)}) %all-gather.8.cloned.1.call-update) | async-done | bytes 2097168 | tf_op jit(solution)/shard_map/all_gather | solution.py:47
  88.2 1.7 reduce.6
  89.9 76.0 %all-gather.10.cloned.1.call-done = f32[4096,128]{1,0:T(8,128)} async-done(((f32[128,128]{1,0:T(8,128)}), f32[4096,128]{1,0:T(8,128)}) %all-gather.10.cloned.1.call-update) | async-done | bytes 2097168 | tf_op jit(solution)/shard_map/all_gather | solution.py:12
  166.0 2.0 convolution_bitcast_fusion
  168.0 1.1 copy.40
  169.1 1.9 fusion.6
  171.0 0.0 copy-start.3
  171.0 5.3 %multiply_reduce_fusion = (f32[6,512]{1,0:T(8,128)S(1)}, f32[6,512,1,128]{1,3,0,2:T(8,128)}) fusion(f32[6,512,1,128]{1,3,0,2:T(8,128)} %fusion.6, f32[6,512,1,128]{1,3,0,2:T(8,128)S(1)} %convolution_bitcast_fusion, bf16[6,512,128]{2,1,0:T(8,128)(2,1)} %bitcast.62, pred[512,512]{1,0:T(8,128)(4,1)S(1)} %iota_compare_fusion, ...), kind=kOutput, calls=%fused_computation.10 | convolution fusion | flops 810021888 | bytes 7355392 | tf_op jit(solution)/shard_map/nhcm,nmhe->nche/dot_general | solution.py:69
  176.3 0.0 copy-done.3
  176.3 1.8 multiply_convert_fusion
  178.1 1.2 copy.29
  179.3 0.0 all-gather.6.cloned.1.call-update
  179.3 74.9 %all-gather.6.cloned.1.call-done = bf16[3072,1024]{1,0:T(8,128)(2,1)} async-done(((bf16[3072,128]{1,0:T(8,128)(2,1)}), bf16[3072,1024]{1,0:T(8,128)(2,1)}) %all-gather.6.cloned.1.call-update) | async-done | bytes 6291472 | tf_op jit(solution)/shard_map/all_gather | solution.py:77
  254.2 0.0 copy-done
  254.2 7.5 %convolution_convert_fusion = bf16[3072,512]{1,0:T(8,128)(2,1)} fusion(bf16[3072,1024]{1,0:T(8,128)(2,1)} %all-gather.6.cloned.1.call-done, bf16[1024,512]{1,0:T(8,128)(2,1)S(1)} %copy-done), kind=kOutput, calls=%fused_computation.2 | convolution fusion | flops 3222798336 | bytes 10485760 | tf_op jit(solution)/shard_map/dot_general | solution.py:76
  (6 shorter events, 0.1 us)
Async XLA Ops:
  6.5 247.6 %copy-start = (bf16[1024,512]{1,0:T(8,128)(2,1)S(1)}, bf16[1024,512]{1,0:T(8,128)(2,1)}, u32[]{:S(2)}) copy-start(bf16[1024,512]{1,0:T(8,128)(2,1)} %param.13) | copy-start | bytes 3145732
  6.5 3.8 %copy-start.1 = (bf16[3072,128]{1,0:T(8,128)(2,1)S(1)}, bf16[3072,128]{1,0:T(8,128)(2,1)}, u32[]{:S(2)}) copy-start(bf16[3072,128]{1,0:T(8,128)(2,1)} %param.10) | copy-start | bytes 2359300
  6.5 3.8 %copy-start.2 = (bf16[3072,128]{1,0:T(8,128)(2,1)S(1)}, bf16[3072,128]{1,0:T(8,128)(2,1)}, u32[]{:S(2)}) copy-start(bf16[3072,128]{1,0:T(8,128)(2,1)} %param.9) | copy-start | bytes 2359300
  6.5 81.7 %all-gather.8.cloned.1.call-start = ((), (), s32[]{:S(2)}) async-start(), calls=%async_computation.1 | async-start | bytes 2162688 | tf_op jit(solution)/shard_map/all_gather | solution.py:47
  10.3 155.7 %all-gather.10.cloned.1.call-start = ((), (), s32[]{:S(2)}) async-start(), calls=%async_computation.2 | async-start | bytes 2162688 | tf_op jit(solution)/shard_map/all_gather | solution.py:12
  11.4 242.8 %all-gather.6.cloned.1.call-start = ((), (), s32[]{:S(2)}) async-start(), calls=%async_computation | async-start | bytes 7077888 | tf_op jit(solution)/shard_map/all_gather | solution.py:77
  171.0 5.3 %copy-start.3 = (f32[128]{0:T(128)S(1)}, f32[128]{0:T(128)}, u32[]{:S(2)}) copy-start(f32[128]{0:T(128)} %param.12) | copy-start | bytes 1540
Sparse Core Ops, SparseCore 0:
  10.4 77.7 all-gather.7
  90.8 75.1 all-gather.9
  179.4 74.7 all-gather.5
